TPU v7x, 256 devices: a whole 4x4x8 slice. The times are simulated.
256 devices in a mesh: ctx: 64 (over y_hi, x, z), heads: 4 (over y_lo, core).
Axes of the slice: x: 4, y: 4 (y_hi: 2, y_lo: 2; y = y_hi * 2 + y_lo), z: 8, core: 2. Of those that a mesh axis runs over, the one named last changes fastest.
Arguments:
- queries: bfloat16 [64, 128, 576], P(None, 'heads'), may hold values from -60 to 60
- latents: bfloat16 [65536, 576], P('ctx'), may hold values from -6 to 6
- index_queries: bfloat16 [64, 64, 128], P(None, 'heads'), may hold values from -24 to 24
- index_keys: bfloat16 [65536, 128], P('ctx'), may hold values from -6 to 6
- index_weights: float32 [64, 64], P(None, 'heads'), may hold values from -15 to 15
- positions: int32 [64], replicated, may hold values from 16384 to 65535, as said below
Outputs:
- grad_index_queries: float32 [64, 64, 128], P(None, 'heads')
- grad_index_keys: float32 [65536, 128], P(('ctx', 'heads'))
Inputs may be any that keep to these rules, and one draw needn't show every extreme that they name: Row q sees keys 0 to positions[q]. One row sits at 65535 and one at 16384.
All inputs are finite; a program needn't handle non-finite values.
Results may differ from a plain program's by a relative error of at most 0.0028.
Values sent between devices are 32-bit elements; how exact they have to be, the bound alone decides.
A program may use at most 64 MiB of HBM per device.

v0:
```python
import math

import jax
import jax.numpy as jnp
from jax import lax
from jax.sharding import PartitionSpec as P

H = 128
HI = 64
DI = 128


score_scale = 192 ** (-0.5)
negative_fill = -1e30


def joined_2(value, axis, combine):
    everything = jax.tree.map(lambda part: lax.all_gather(part, axis), value)
    leading = jax.tree.map(lambda part: part[0], everything)

    def turn(k, so_far):
        return combine(so_far, jax.tree.map(lambda part: part[k], everything))

    return lax.fori_loop(1, lax.axis_size(axis), turn, leading)


def combine_stats(former, latter):
    joined = jnp.maximum(former[0], latter[0])
    return (
        joined,
        former[1] * jnp.exp(former[0] - joined) + latter[1] * jnp.exp(latter[0] - joined),
    )


def masked_scores(block_queries, latents, block_visible):
    row_count, head_count, width = block_queries.shape
    flattened = block_queries.reshape(row_count * head_count, width)
    products = lax.dot_general(
        flattened, latents, (((1,), (1,)), ((), ())), preferred_element_type=jnp.float32
    )
    products = products.reshape(row_count, head_count, -1) * score_scale
    return jnp.where(block_visible[:, None, :], products, negative_fill)


def local_stats(logits, visible_now):
    masked = jnp.where(visible_now, logits, negative_fill)
    row_peak = jnp.max(masked, axis=1)
    row_mass = jnp.sum(jnp.where(visible_now, jnp.exp(masked - row_peak[:, None]), 0.0), axis=1)
    return (masked, row_peak, row_mass)


def gradient_of(masked, visible_now, row_peak, row_mass, target_sum, loss_scale):
    index_probs = jnp.where(
        visible_now, jnp.exp(masked - row_peak[:, None]) / row_mass[:, None], 0.0
    )
    return loss_scale * (index_probs - target_sum * (1.0 / H))


def body(queries, latents, index_queries, index_keys, index_weights, positions):
    row_count, heads_local, width = queries.shape
    keys_local = latents.shape[0]
    ctx_count = lax.axis_size("ctx")
    loss_scale = float(ctx_count * keys_local // 64)
    key_pos = lax.axis_index("ctx") * keys_local + lax.iota(jnp.int32, keys_local)
    visible = key_pos[None, :] <= positions[:, None]
    block_rows = math.gcd(row_count, max(1, 512 // heads_local))
    nblocks = row_count // block_rows
    query_blocks = queries.reshape(nblocks, block_rows, heads_local, width)
    visible_blocks = visible.reshape(nblocks, block_rows, keys_local)

    def first_pass(inputs):
        scores = masked_scores(inputs[0], latents, inputs[1])
        local_max = jnp.max(scores, axis=2)
        local_total = jnp.sum(
            jnp.where(inputs[1][:, None, :], jnp.exp(scores - local_max[:, :, None]), 0.0), axis=2
        )
        return (scores, local_max, local_total)

    stored, local_max, local_total = lax.map(first_pass, (query_blocks, visible_blocks))
    local_max = local_max.reshape(row_count, heads_local)
    local_total = local_total.reshape(row_count, heads_local)
    index_local = index_queries.shape[1]
    flat_index = index_queries.reshape(row_count * index_local, -1)
    index_dots = lax.dot_general(
        flat_index, index_keys, (((1,), (1,)), ((), ())), preferred_element_type=jnp.float32
    )
    index_dots = index_dots.reshape(row_count, index_local, keys_local)
    scaled_weights = index_weights * (HI * DI) ** (-0.5)
    logit_part = jnp.sum(scaled_weights[:, :, None] * jnp.maximum(index_dots, 0.0), axis=1)
    row_max = lax.pmax(local_max, "ctx")
    row_total = lax.psum(local_total * jnp.exp(local_max - row_max), "ctx")
    max_blocks = row_max.reshape(nblocks, block_rows, heads_local)
    total_blocks = row_total.reshape(nblocks, block_rows, heads_local)

    def second_pass(inputs):
        source, block_visible, block_max, block_total = inputs
        weights_now = jnp.where(
            block_visible[:, None, :],
            jnp.exp(source - block_max[:, :, None]) / block_total[:, :, None],
            0.0,
        )
        return jnp.sum(weights_now, axis=1)

    target_part = lax.map(second_pass, (stored, visible_blocks, max_blocks, total_blocks)).reshape(
        row_count, keys_local
    )
    target_sum, logit_sum = lax.psum((target_part, logit_part), "heads")
    masked, row_peak, row_mass = local_stats(logit_sum, visible)
    row_peak, row_mass = joined_2((row_peak, row_mass), "ctx", combine_stats)
    logit_grad = gradient_of(masked, visible, row_peak, row_mass, target_sum, loss_scale)
    coefficient = jnp.where(
        index_dots > 0.0, logit_grad[:, None, :] * scaled_weights[:, :, None], 0.0
    )
    flat_coefficient = coefficient.astype(jnp.bfloat16).reshape(row_count * index_local, keys_local)
    query_part = jnp.dot(flat_coefficient, index_keys, preferred_element_type=jnp.float32)
    grad_queries = lax.psum(query_part, "ctx").reshape(row_count, index_local, -1)
    grad_keys = lax.psum_scatter(
        lax.dot_general(
            flat_coefficient,
            flat_index,
            (((0,), (0,)), ((), ())),
            preferred_element_type=jnp.float32,
        ),
        "heads",
        scatter_dimension=0,
        tiled=True,
    )
    return (grad_queries, grad_keys)


def solution(mesh):
    placed = (
        P(None, "heads", None),
        P("ctx", None),
        P(None, "heads", None),
        P("ctx", None),
        P(None, "heads"),
        P(),
    )
    return jax.shard_map(
        body,
        mesh=mesh,
        in_specs=placed,
        out_specs=(P(None, "heads", None), P(("ctx", "heads"), None)),
        check_vma=False,
    )
```

profile of v0, /device:TPU:8, one launch (start us, length us, event | category | flops | bytes accessed | tf_op | source)
XLA Modules:
  0.0 1534.3 jit_solution(12108102114537619191)
XLA Ops:
  7.2 0.0 all-reduce.7.cloned.1.call-start
  7.2 0.7 broadcast_multiply_fusion
  8.0 0.1 copy.8
  8.0 0.1 copy-done
  8.1 4.7 multiply_reduce_fusion
  12.8 0.0 all-reduce.9.cloned.1.call-start
  12.9 0.1 le.26
  13.0 0.7 broadcast_compare_fusion
  13.8 27.8 %while.42 = (s32[]{:T(128)}, f32[4,16,32,1024]{3,2,1,0:T(8,128)}, f32[4,16,32]{2,1,0:T(8,128)}, f32[4,16,32]{2,1,0:T(8,128)}, pred[4,16,1024]{2,1,0:T(8,128)(4,1...) while((s32[]{:T(128)}, f32[4,16,32,1024]{3,2,1,0:T(8,128)}, ...), condition=%wide.region_9.10_spmd, body=%wide.region_6.9_spmd.sunk | while | flops 607124480 | bytes 10325633 | solution.py:79
  13.8 0.7 dynamic-slice_bitcast_fusion.7
  14.5 3.5 bitcast_dynamic-update-slice_fusion.7
  18.0 0.8 reduce_max.21
  18.8 1.3 select_reduce_fusion.2
  20.1 0.6 bitcast_dynamic-update-slice_fusion.8
  20.7 0.7 dynamic-slice_bitcast_fusion.7
  21.5 3.5 bitcast_dynamic-update-slice_fusion.7
  24.9 0.8 reduce_max.21
  25.7 1.3 select_reduce_fusion.2
  27.0 0.6 bitcast_dynamic-update-slice_fusion.8
  27.6 0.7 dynamic-slice_bitcast_fusion.7
  28.4 3.5 bitcast_dynamic-update-slice_fusion.7
  31.9 0.8 reduce_max.21
  32.6 1.3 select_reduce_fusion.2
  34.0 0.6 bitcast_dynamic-update-slice_fusion.8
  34.6 0.7 dynamic-slice_bitcast_fusion.7
  35.3 3.5 bitcast_dynamic-update-slice_fusion.7
  38.8 0.8 reduce_max.21
  39.6 1.3 select_reduce_fusion.2
  40.9 0.6 bitcast_dynamic-update-slice_fusion.8
  41.6 1.3 dynamic-slice
  43.5 360.6 %pmax.7 = f32[64,32]{1,0:T(8,128)S(1)} all-reduce(f32[64,32]{1,0:T(8,128)} %bitcast.96), channel_id=1, replica_groups=mesh['ctx'=64,'heads'=4] {'ctx'}, use_global_device_ids=true, to_apply=%region_10.11 | all-reduce | flops 2048 | bytes 16384 | tf_op jit(solution)/shard_map/pmax | solution.py:90
  404.1 0.8 bitcast_multiply_fusion.1
  404.9 0.0 all-reduce.7.cloned.1.call-done
  404.9 1.2 fusion.15
  406.1 0.3 dynamic-update-slice
  406.4 1.2 fusion.10
  407.6 0.3 dynamic-update-slice.1
  407.9 350.9 %all-reduce.2 = (f32[4,16,32]{2,1,0:T(8,128)S(1)}, f32[4096]{0:T(1024)S(1)}, f32[4096]{0:T(1024)S(1)}) all-reduce(f32[4,16,32]{2,1,0:T(8,128)S(1)} %bitcast.97, f32[4096]{0:T(1024)S(1)} %dynamic-update-slice, f32[4096]{0:T(1024)S(1)} %dynamic-update-slice.1), channel_id=1, replica_groups=mesh['ctx'=64,'heads'=4] {'ctx'}, use_global_device_ids=true, to_apply=%region_11.12 | all-reduce | flops 10240 | bytes 81920 | tf_op jit(solution)/shard_map/psum | solution.py:91
  758.8 0.1 reshape.74
  758.9 0.1 reshape.75
  758.9 15.4 %while.43 = (s32[]{:T(128)}, f32[4,16,1024]{2,1,0:T(8,128)}, pred[4,16,1024]{2,1,0:T(8,128)(4,1)}, f32[4,16,32,1024]{3,2,1,0:T(8,128)}, f32[4,16,32]{2,1,0:T(8,128)S(1)}, /*index=5*/f32[4,16,32]{2,1,0:T(8,128)S(1)}, s32[]{:T(128)}) while((s32[]{:T(128)}, f32[4,16,1024]{2,1,0:T(8,128)}, pred[4,16,1024]{2,1,0:T(8,128)(4,1)}, ...), condition=%wide.region_14.15_spmd, body=%wide.region_12.14_spmd.sunk | while | flops 2080770 | bytes 2355801 | solution.py:104
  759.0 0.8 dynamic-slice_bitcast_fusion.9
  759.7 2.5 fusion.25
  762.2 0.6 bitcast_dynamic-update-slice_fusion.9
  762.8 0.7 dynamic-slice_bitcast_fusion.9
  763.6 2.5 fusion.25
  766.0 0.6 bitcast_dynamic-update-slice_fusion.9
  766.7 0.7 dynamic-slice_bitcast_fusion.9
  767.4 2.5 fusion.25
  769.9 0.6 bitcast_dynamic-update-slice_fusion.9
  770.5 0.7 dynamic-slice_bitcast_fusion.9
  771.2 2.5 fusion.25
  773.7 0.6 bitcast_dynamic-update-slice_fusion.9
  774.4 0.0 all-reduce.11.cloned.1.call-start
  774.4 2.9 while.41
  777.3 30.8 %all-reduce.9.cloned.1.call-done = f32[64,1024]{1,0:T(8,128)} async-done(((f32[64,1024]{1,0:T(8,128)}), f32[64,1024]{1,0:T(8,128)}) %all-reduce.9.cloned.1.call-update) | async-done | bytes 262160 | tf_op jit(solution)/shard_map/psum | solution.py:107
  808.0 1.1 fusion.12
  809.2 2.8 select_convert_fusion
  811.9 1.5 fusion.16
  813.5 0.0 reduce-scatter.2.cloned.1.call-start
  813.5 1.5 convolution_bitcast_fusion
  815.1 690.0 %all-reduce.11.cloned.1.call-done = f32[64,16,128]{2,1,0:T(8,128)} async-done(((f32[64,16,128]{2,1,0:T(8,128)}), f32[64,16,128]{2,1,0:T(8,128)}) %all-reduce.11.cloned.1.call-update) | async-done | bytes 524304 | tf_op jit(solution)/shard_map/psum | solution.py:116
  1505.1 20.8 %reduce-scatter.2.cloned.1.call-done = f32[256,128]{1,0:T(8,128)} async-done(((f32[1024,128]{1,0:T(8,128)}), f32[256,128]{1,0:T(8,128)}) %reduce-scatter.2.cloned.1.call-update) | async-done | bytes 131088 | tf_op jit(solution)/shard_map/reduce_scatter | solution.py:117
  1525.9 1.9 copy.49
  (107 shorter events, 1.9 us)
Async XLA Ops:
  7.2 1.0 copy-start
  7.2 397.8 %all-reduce.7.cloned.1.call-start = ((), (), s32[]{:S(2)}) async-start(), calls=%async_computation.1 | async-start | bytes 524288 | tf_op jit(solution)/shard_map/psum | solution.py:107
  8.1 4.7 copy-start.4
  8.1 4.8 copy-start.9
  8.1 5.6 copy-start.1
  12.8 795.2 %all-reduce.9.cloned.1.call-start = ((), (), s32[]{:S(2)}) async-start(), calls=%async_computation.2 | async-start | bytes 524288 | tf_op jit(solution)/shard_map/psum | solution.py:107
  12.9 0.8 copy-start.7
  18.8 1.4 copy-start.3
  25.7 1.4 copy-start.3
  32.6 1.4 copy-start.3
  39.6 1.4 copy-start.3
  758.9 49.1 %copy-start.2 = (f32[64,1024]{1,0:T(8,128)S(1)}, f32[64,1024]{1,0:T(8,128)}, u32[]{:S(2)}) copy-start(f32[64,1024]{1,0:T(8,128)} %all-reduce.7.cloned.1.call-done) | copy-start | bytes 786436
  758.9 49.1 %copy-start.8 = (s32[1024]{0:T(1024)S(1)}, s32[1024]{0:T(1024)}, u32[]{:S(2)}) copy-start(s32[1024]{0:T(1024)} %copy-done.7) | copy-start | bytes 12292
  758.9 49.1 %copy-start.10 = (s32[64]{0:T(128)S(1)}, s32[64]{0:T(128)}, u32[]{:S(2)}) copy-start(s32[64]{0:T(128)} %param.17) | copy-start | bytes 772
  758.9 50.2 %copy-start.5 = (f32[64,16]{1,0:T(8,128)S(1)}, f32[64,16]{1,0:T(8,128)}, u32[]{:S(2)}) copy-start(f32[64,16]{1,0:T(8,128)} %copy-done.4) | copy-start | bytes 12292
  774.4 730.8 %all-reduce.11.cloned.1.call-start = ((), (), s32[]{:S(2)}) async-start(), calls=%async_computation.3 | async-start | bytes 1048576 | tf_op jit(solution)/shard_map/psum | solution.py:116
  811.9 1.6 copy-start.6
  813.5 712.4 %reduce-scatter.2.cloned.1.call-start = ((), (), s32[]{:S(2)}) async-start(), calls=%async_computation.4 | async-start | bytes 655360 | tf_op jit(solution)/shard_map/reduce_scatter | solution.py:117
Sparse Core Ops, SparseCore 0:
  12.9 43.3 all-reduce.6
  774.5 33.4 all-reduce.8
  813.6 691.4 all-reduce.10
  1508.3 17.5 reduce-scatter.1
where the time goes:
time: 1540 us; the launch traced here: 1530 us
  waiting for transfers between devices  742 us (48%)
  blocking collectives  712 us (46%)
  other arithmetic  28.6 us (2%)
  matrix products  21.7 us (1%)
    psum x1, waiting for transfers between devices, body(): lax.psum(query_part, 'ctx').reshape(row_count, index_local, -1)  690 us
    pmax x1, blocking collectives, body(): row_max = lax.pmax(local_max, 'ctx')  361 us
    psum x1, blocking collectives, body(): row_total = lax.psum(local_total * jnp.exp(local_max - row_max), 'ctx')  351 us
  transfers between devices with their start and end apart: 4, of which 3 were waited for; matrix products, arithmetic and copies ran while one was open for 2% of the time, Pallas kernels for 0%

commit v1 on v0

v1 whole, which is shorter than its diff:
```python
import functools

import jax
import jax.numpy as jnp
from jax import lax
from jax.experimental import pallas as pl
from jax.experimental.pallas import tpu as pltpu
from jax.sharding import PartitionSpec as P

MESH = pl.DeviceIdType.MESH
F32 = jnp.float32
BF16 = jnp.bfloat16

Q, H, HI, DI = 64, 128, 64, 128
NZ = 8
NG = 8
HL = 32
JL = 16
KEYS = 1024
QB = 8
NB = Q // QB
LOG2E = 1.4426950408889634
SCORE_SCALE = (192 ** (-0.5)) * LOG2E
INDEX_SCALE = (HI * DI) ** (-0.5)
FILL = -1e30
LOSS_SCALE = 1024.0


def kernel(
    pos_ref, q_ref, lat_ref, iq_ref, ik_ref, wt_ref,
    gq_ref, gk_ref,
    prod, ex, iqf, iqp, iqt, ikt, dots, wpad, w_ref, coef,
    lg, lg_rc, lg_ry, lg_fin,
    tg, tg_rc, tg_ry, tg_fin,
    st, st_rz, st2, st_rx, fac,
    gq_tmp, gq, gq_rx, gq_s1, gq_rz, blk,
    gk_p, gk_rc, gk_s, gk_ry,
    pair_send, pair_recv, send_z, recv_z, send_x, recv_x,
):
    c = lax.axis_index("ctx")
    h = lax.axis_index("heads")
    z, g = c % NZ, c // NZ
    core, ylo = h % 2, h // 2
    core_peer = (c, ylo * 2 + (1 - core))
    ylo_peer = (c, (1 - ylo) * 2 + core)
    far = (4, 3, 5, 2, 6, 1, 7)
    z_ids = [(z + k) % NZ for k in far]
    g_ids = [(g + k) % NG for k in far]
    z_peers = [(g * NZ + i, h) for i in z_ids]
    g_peers = [(i * NZ + z, h) for i in g_ids]
    peers = z_peers + g_peers + [core_peer, ylo_peer]

    barrier = pltpu.get_barrier_semaphore()
    for p in peers:
        pl.semaphore_signal(barrier, inc=1, device_id=p, device_id_type=MESH)

    def remote(src, dst, send, recv, peer):
        return pltpu.make_async_remote_copy(
            src_ref=src, dst_ref=dst, send_sem=send, recv_sem=recv,
            device_id=peer, device_id_type=MESH,
        )

    def pair(slot, src, dst, peer):
        return remote(src, dst, pair_send.at[slot], pair_recv.at[slot], peer)

    iqf[...] = iq_ref[...].astype(F32)

    def permute(b, _):
        for j in range(0, JL, 2):
            two = [iqf[pl.ds(b * 128 + j + i, QB, stride=JL), :] for i in range(2)]
            iqp[pl.ds(b * 128 + j * QB, 2 * QB), :] = jnp.concatenate(two, axis=0).astype(BF16)
        return 0

    lax.fori_loop(0, NB, permute, 0)
    ikt[...] = ik_ref[...].T
    iqt[...] = iqp[...].T
    wpad[...] = jnp.zeros_like(wpad)
    wpad[0:JL, 0:Q] = wt_ref[...] * INDEX_SCALE
    w_ref[...] = wpad[...].T

    key_pos = c * KEYS + lax.broadcasted_iota(jnp.int32, (QB, KEYS), 1)
    row_iota = lax.broadcasted_iota(jnp.int32, (QB, 1), 0)
    lane = lax.broadcasted_iota(jnp.int32, (QB, 128), 1)

    def visible_of(b):
        col = jnp.zeros((QB, 1), jnp.int32)
        for i in range(QB):
            col = jnp.where(row_iota == i, pos_ref[b * QB + i], col)
        return key_pos <= col

    def index_block(b, _):
        rows = pl.ds(pl.multiple_of(b * 128, 128), 128)
        dots[rows, :] = jnp.dot(iqp[rows, :], ikt[...], preferred_element_type=F32)
        wb = w_ref[pl.ds(pl.multiple_of(b * QB, QB), QB), :]
        total = jnp.zeros((QB, KEYS), F32)
        for j in range(JL):
            d = dots[pl.ds(pl.multiple_of(b * 128 + j * QB, QB), QB), :]
            total = total + wb[:, j : j + 1] * jnp.maximum(d, 0.0)
        lg[pl.ds(pl.multiple_of(b * QB, QB), QB), :] = jnp.where(visible_of(b), total, FILL)
        return 0

    lax.fori_loop(0, NB, index_block, 0)

    def attention_block(b, _):
        rows = pl.ds(pl.multiple_of(b * (QB * HL), QB * HL), QB * HL)
        for n in range(KEYS // 256):
            part = jnp.dot(
                q_ref[rows, :], lat_ref[:, n * 256 : (n + 1) * 256], preferred_element_type=F32
            )
            prod[2 * n] = part[:, :128]
            prod[2 * n + 1] = part[:, 128:]
        vis = visible_of(b)
        first = HL * (b % 4)
        group = pl.ds(pl.multiple_of(QB * (b // 4), QB), QB)
        group2 = pl.ds(pl.multiple_of(16 + QB * (b // 4), QB), QB)

        def head(k, carry):
            ms, ls = carry
            x = jnp.concatenate(
                [prod[n, pl.ds(k, QB, stride=HL), :] for n in range(KEYS // 128)], axis=1
            )
            x = jnp.where(vis, x * SCORE_SCALE, FILL)
            m = jnp.max(x, axis=1, keepdims=True)
            e = jnp.exp2(x - m)
            l = jnp.sum(e, axis=1, keepdims=True)
            ex[pl.ds(pl.multiple_of(b * (QB * HL) + k * QB, QB), QB), :] = e
            here = lane == first + k
            return jnp.where(here, m, ms), jnp.where(here, l, ls)

        ms, ls = lax.fori_loop(0, HL, head, (st[group, :], st[group2, :]), unroll=True)
        st[group, :] = ms
        st[group2, :] = ls
        return 0

    st[...] = jnp.zeros_like(st)
    half = pl.ds(pl.multiple_of(core * 32, 32), 32)
    other = pl.ds(pl.multiple_of((1 - core) * 32, 32), 32)

    lax.fori_loop(0, 2, attention_block, 0)
    pl.semaphore_wait(barrier, len(peers))
    c1 = pair(0, lg.at[other], lg_rc, core_peer)
    c1.start()
    lax.fori_loop(2, 4, attention_block, 0)
    c1.wait()
    lg[half, :] = lg[half, :] + lg_rc[...]
    c2 = pair(1, lg.at[half], lg_ry, ylo_peer)
    c2.start()
    lax.fori_loop(4, 7, attention_block, 0)
    c2.wait()
    lg_fin[half, :] = lg[half, :] + lg_ry[...]
    c3 = pair(2, lg_fin.at[half], lg_fin.at[half], core_peer)
    c3.start()
    lax.fori_loop(7, 8, attention_block, 0)
    c3.wait()

    def index_stats(b, ix):
        x = lg_fin[pl.ds(pl.multiple_of(b * QB, QB), QB), :] * LOG2E
        m = jnp.max(x, axis=1, keepdims=True)
        l = jnp.sum(jnp.exp2(x - m), axis=1, keepdims=True)
        return jnp.where(lane == b, m, jnp.where(lane == b + 64, l, ix))

    st[32:40, :] = lax.fori_loop(0, NB, index_stats, jnp.zeros((QB, 128), F32))

    def exchange(src, dst, sends, recvs, targets):
        copies = [remote(src, dst.at[k], sends.at[k], recvs.at[k], p) for k, p in enumerate(targets)]
        for copy in copies:
            copy.start()
        for copy in copies:
            copy.wait()

    def combine(own, received):
        parts = [own[...]] + [received[k] for k in range(7)]
        top = functools.reduce(jnp.maximum, [p[0:16] for p in parts])
        mass = sum(p[16:32] * jnp.exp2(p[0:16] - top) for p in parts)
        peak = functools.reduce(jnp.maximum, [p[32:40] for p in parts])
        low = lane < 64
        imass = sum(
            p[32:40] * pltpu.roll(jnp.exp2(jnp.where(low, p[32:40] - peak, 0.0)), 64, 1)
            for p in parts
        )
        return top, mass, jnp.where(low, peak, imass)

    exchange(st, st_rz, send_z.at[0], recv_z.at[0], z_peers)
    top, mass, idx = combine(st, st_rz)
    st2[0:16, :] = top
    st2[16:32, :] = mass
    st2[32:40, :] = idx
    exchange(st2, st_rx, send_x.at[0], recv_x.at[0], g_peers)
    top, mass, idx = combine(st2, st_rx)
    fac[0:16, :] = jnp.exp2(st[0:16, :] - top) / mass
    fac[16:24, :] = idx

    def target_block(b, _):
        f = fac[pl.ds(pl.multiple_of(QB * (b // 4), QB), QB), :]
        f = pltpu.roll(f, (128 - HL * (b % 4)) % 128, 1)
        total = jnp.zeros((QB, KEYS), F32)
        for k in range(HL):
            e = ex[pl.ds(pl.multiple_of(b * (QB * HL) + k * QB, QB), QB), :]
            total = total + e * f[:, k : k + 1]
        tg[pl.ds(pl.multiple_of(b * QB, QB), QB), :] = total
        return 0

    lax.fori_loop(0, NB, target_block, 0)
    c4 = pair(3, tg.at[other], tg_rc, core_peer)
    c4.start()
    c4.wait()
    tg[half, :] = tg[half, :] + tg_rc[...]
    c5 = pair(4, tg.at[half], tg_ry, ylo_peer)
    c5.start()
    c5.wait()
    tg_fin[half, :] = tg[half, :] + tg_ry[...]
    c6 = pair(5, tg_fin.at[half], tg_fin.at[half], core_peer)
    c6.start()
    c6.wait()

    def grad_block(b):
        rows = pl.ds(pl.multiple_of(b * QB, QB), QB)
        ix = fac[16:24, :]
        peak = jnp.sum(jnp.where(lane == b, ix, 0.0), axis=1, keepdims=True)
        mass = jnp.sum(jnp.where(lane == b + 64, ix, 0.0), axis=1, keepdims=True)
        probs = jnp.exp2(lg_fin[rows, :] * LOG2E - peak) * (1.0 / mass)
        grad = LOSS_SCALE * (probs - tg_fin[rows, :] * (1.0 / H))
        wb = w_ref[rows, :]
        for j in range(0, JL, 2):
            two = []
            for i in (j, j + 1):
                d = dots[pl.ds(pl.multiple_of(b * 128 + i * QB, QB), QB), :]
                two.append(jnp.where(d > 0.0, grad * wb[:, i : i + 1], 0.0))
            at = pl.ds(pl.multiple_of(b * 128 + j * QB, 2 * QB), 2 * QB)
            coef[at, :] = jnp.concatenate(two, axis=0).astype(BF16)
        here = pl.ds(pl.multiple_of(b * 128, 128), 128)
        gq_tmp[...] = jnp.dot(coef[here, :], ik_ref[...], preferred_element_type=F32)
        for i in range(QB):
            gq[b, pl.ds(i * JL, JL), :] = gq_tmp[pl.ds(i, JL, stride=QB), :]

    def grad_send(k, _):
        b = (g + 1 + k) % NG
        grad_block(b)
        remote(
            gq.at[b], gq_rx.at[k], send_x.at[1, k], recv_x.at[1, k], (b * NZ + z, h)
        ).start()
        return 0

    lax.fori_loop(0, 7, grad_send, 0)
    grad_block(g)

    for piece in range(4):
        gk_p[piece % 2, piece // 2] = jnp.dot(
            iqt[...], coef[:, piece * 256 : (piece + 1) * 256], preferred_element_type=F32
        )
    c7 = pair(6, gk_p.at[1 - core], gk_rc, core_peer)
    c7.start()
    c7.wait()
    gk_s[...] = gk_p[core] + gk_rc[...]
    c8 = pair(7, gk_s.at[1 - ylo], gk_ry, ylo_peer)
    c8.start()

    total = gq[g]
    for k in range(7):
        copy = remote(
            gq.at[(g + 1 + k) % NG], gq_rx.at[k], send_x.at[1, k], recv_x.at[1, k],
            (((g + 1 + k) % NG) * NZ + z, h),
        )
        copy.wait()
        total = total + gq_rx[k]
    gq_s1[...] = total.reshape(NZ, JL, DI)
    copies = [
        remote(gq_s1.at[i], gq_rz.at[k], send_z.at[1, k], recv_z.at[1, k], p)
        for k, (i, p) in enumerate(zip(z_ids, z_peers))
    ]
    for copy in copies:
        copy.start()
    for copy in copies:
        copy.wait()
    total = gq_s1[z]
    for k in range(7):
        total = total + gq_rz[k]
    blk[z] = total
    copies = [
        remote(blk.at[z], blk.at[z], send_z.at[2, k], recv_z.at[2, k], p)
        for k, p in enumerate(z_peers)
    ]
    for copy in copies:
        copy.start()
    c8.wait()
    gk_ref[...] = (gk_s[ylo] + gk_ry[...]).T
    for copy in copies:
        copy.wait()
    mine = gq_ref.at[pl.ds(pl.multiple_of(g * 128, 128), 128)]
    gq_ref[pl.ds(pl.multiple_of(g * 128, 128), 128), :] = blk[...].reshape(128, DI)
    copies = [
        remote(mine, mine, send_x.at[2, k], recv_x.at[2, k], p) for k, p in enumerate(g_peers)
    ]
    for copy in copies:
        copy.start()
    for copy in copies:
        copy.wait()


def body(queries, latents, index_queries, index_keys, index_weights, positions):
    vmem = pl.BlockSpec(memory_space=pltpu.VMEM)
    smem = pl.BlockSpec(memory_space=pltpu.SMEM)
    rows = Q * HL
    v = pltpu.VMEM
    dma = pltpu.SemaphoreType.DMA
    scratch = [
        v((KEYS // 128, QB * HL, 128), F32),
        v((rows, KEYS), F32),
        v((Q * JL, DI), F32),
        v((Q * JL, DI), BF16),
        v((DI, Q * JL), BF16),
        v((DI, KEYS), BF16),
        v((Q * JL, KEYS), F32),
        v((128, 128), F32),
        v((128, 128), F32),
        v((Q * JL, KEYS), BF16),
    ]
    for _ in range(2):
        scratch += [v((Q, KEYS), F32), v((32, KEYS), F32), v((32, KEYS), F32), v((Q, KEYS), F32)]
    scratch += [
        v((40, 128), F32), v((7, 40, 128), F32), v((40, 128), F32), v((7, 40, 128), F32),
        v((24, 128), F32),
        v((128, DI), F32), v((NB, 128, DI), F32), v((7, 128, DI), F32), v((NZ, JL, DI), F32),
        v((7, JL, DI), F32), v((NZ, JL, DI), F32),
        v((2, 2, DI, 256), F32), v((2, DI, 256), F32), v((2, DI, 256), F32), v((DI, 256), F32),
        dma((8,)), dma((8,)), dma((3, 7)), dma((3, 7)), dma((3, 7)), dma((3, 7)),
    ]
    grad_queries, grad_keys = pl.pallas_call(
        kernel,
        out_shape=(
            jax.ShapeDtypeStruct((Q * JL, DI), F32),
            jax.ShapeDtypeStruct((KEYS // 4, DI), F32),
        ),
        in_specs=[smem] + [vmem] * 5,
        out_specs=(vmem, vmem),
        scratch_shapes=scratch,
        compiler_params=pltpu.CompilerParams(
            collective_id=0, has_side_effects=True, vmem_limit_bytes=48 * 1024 * 1024
        ),
    )(
        positions,
        queries.reshape(rows, queries.shape[2]),
        latents.T,
        index_queries.reshape(Q * JL, DI),
        index_keys,
        index_weights.T,
    )
    return grad_queries.reshape(Q, JL, DI), grad_keys


def solution(mesh):
    placed = (
        P(None, "heads", None),
        P("ctx", None),
        P(None, "heads", None),
        P("ctx", None),
        P(None, "heads"),
        P(),
    )
    return jax.shard_map(
        body,
        mesh=mesh,
        in_specs=placed,
        out_specs=(P(None, "heads", None), P(("ctx", "heads"), None)),
        check_vma=False,
    )
```

time: 1540 us -> 80.4 us (0.05)
  waiting for transfers between devices: 742 us -> 0 us
  blocking collectives: 712 us -> 0 us
  Pallas kernels: 0 us -> 71.8 us
  other arithmetic: 28.6 us -> 0 us
  matrix products: 21.7 us -> 0 us
    psum x3 -> x0, waiting for transfers between devices: 721 us -> none  [the longest x1 690 us: body(): lax.psum(query_part, 'ctx').reshape(row_count, index_local, -1)]
    pmax x1 -> x0, blocking collectives: 361 us -> none  [body(): row_max = lax.pmax(local_max, 'ctx')]
    psum x1 -> x0, blocking collectives: 351 us -> none  [body(): row_total = lax.psum(local_total * jnp.exp(local_max - row_max), 'ctx')]
    pallas_call x0 -> x1, Pallas kernels: none -> 71.8 us  [body(): pl.pallas_call(kernel, out_shape=(jax.ShapeDtypeStruct((Q * JL, DI), F32)...]
    dot_general x7 -> x0, matrix products: 21.7 us -> none  [the longest x4 14 us: masked_scores(): lax.dot_general(flattened, latents, (((1,), (1,)), ((), ())), preferred_e...]
    reduce_scatter x1 -> x0, waiting for transfers between devices: 20.8 us -> none  [body(): lax.psum_scatter(lax.dot_general(flat_coefficient, flat_index, (((0,), (0...]
    reduce_sum x9 -> x0, other arithmetic: 16.5 us -> none  [the longest x4 9.88 us: second_pass(): return jnp.sum(weights_now, axis=1)]
  transfers between devices with their start and end apart: 4 -> 0, of which waited for: 3 -> 0; matrix products, arithmetic and copies ran while one was open for 2% -> 0% of each run, Pallas kernels for 0% -> 0%
where the time goes in v1:
time: 80.4 us; the launch traced here: 80.1 us
  Pallas kernels  71.8 us (89%)
  local copies, waits for them, and re-layouts  7.7 us (10%)
    pallas_call x1, Pallas kernels, body(): pl.pallas_call(kernel, out_shape=(jax.ShapeDtypeStruct((Q * JL, DI), F32)...  71.8 us
    unnamed x14, local copies, waits for them, and re-layouts  7.7 us

profile of v1, /device:TPU:8, one launch (start us, length us, event | category | flops | bytes accessed | tf_op | source)
XLA Modules:
  0.0 80.1 jit_solution(4346958687919798057)
XLA Ops:
  0.6 0.0 copy-start
  0.6 1.7 %copy-done = bf16[64,32,576]{2,1,0:T(8,128)(2,1)S(1)} copy-done((bf16[64,32,576]{2,1,0:T(8,128)(2,1)S(1)}, bf16[64,32,576]{2,1,0:T(8,128)(2,1)}, u32[]{:S(2)}) %copy-start) | copy-done | bytes 2359320
  2.4 0.0 copy-start.1
  2.4 1.3 %copy-done.1 = bf16[1024,576]{0,1:T(8,128)(2,1)S(1)} copy-done((bf16[1024,576]{0,1:T(8,128)(2,1)S(1)}, bf16[1024,576]{0,1:T(8,128)(2,1)}, u32[]{:S(2)}) %copy-start.1) | copy-done | bytes 1179672
  3.6 0.0 copy-start.2
  3.6 0.9 %copy-done.2 = bf16[64,16,128]{2,1,0:T(8,128)(2,1)S(1)} copy-done((bf16[64,16,128]{2,1,0:T(8,128)(2,1)S(1)}, bf16[64,16,128]{2,1,0:T(8,128)(2,1)}, u32[]{:S(2)}) %copy-start.2) | copy-done | bytes 262168
  4.6 0.0 copy-start.3
  4.6 0.9 %copy-done.3 = bf16[1024,128]{1,0:T(8,128)(2,1)S(1)} copy-done((bf16[1024,128]{1,0:T(8,128)(2,1)S(1)}, bf16[1024,128]{1,0:T(8,128)(2,1)}, u32[]{:S(2)}) %copy-start.3) | copy-done | bytes 262168
  5.5 0.0 copy-start.4
  5.5 0.7 copy-done.4
  6.2 0.0 copy-start.5
  6.2 0.7 copy-done.5
  6.9 71.8 %shard_map.77 = (f32[1024,128]{1,0:T(8,128)S(1)}, f32[256,128]{1,0:T(8,128)S(1)}) custom-call(s32[64]{0:T(128)S(1)} %copy-done.5, bf16[2048,576]{1,0:T(8,128)(2,1)S(1)} %bitcast.5, bf16[576,1024]{1,0:T(8,128)(2,1)S(1)} %bitcast.6, bf16[1024,128]{1,0:T(8,128)(2,1)S(1)} %bitcast.8, bf16[1024,128]{1,0:T(8,128)(2,1)S(1)} %copy-done.3, f32[16,64]{1,0:T(8,128)S(1)} %bitcast.9), custom_call_target="tpu_custom_call" | custom-call | tf_op jit(solution)/shard_map/pallas_call | solution.py:328
  78.7 0.8 copy.10
  79.5 0.7 copy.11
Async XLA Ops:
  0.6 1.7 %copy-start = (bf16[64,32,576]{2,1,0:T(8,128)(2,1)S(1)}, bf16[64,32,576]{2,1,0:T(8,128)(2,1)}, u32[]{:S(2)}) copy-start(bf16[64,32,576]{2,1,0:T(8,128)(2,1)} %param.6) | copy-start | bytes 7077892
  2.4 1.3 %copy-start.1 = (bf16[1024,576]{0,1:T(8,128)(2,1)S(1)}, bf16[1024,576]{0,1:T(8,128)(2,1)}, u32[]{:S(2)}) copy-start(bf16[1024,576]{0,1:T(8,128)(2,1)} %param.7) | copy-start | bytes 3538948
  3.6 0.9 %copy-start.2 = (bf16[64,16,128]{2,1,0:T(8,128)(2,1)S(1)}, bf16[64,16,128]{2,1,0:T(8,128)(2,1)}, u32[]{:S(2)}) copy-start(bf16[64,16,128]{2,1,0:T(8,128)(2,1)} %param.8) | copy-start | bytes 786436
  4.6 0.9 %copy-start.3 = (bf16[1024,128]{1,0:T(8,128)(2,1)S(1)}, bf16[1024,128]{1,0:T(8,128)(2,1)}, u32[]{:S(2)}) copy-start(bf16[1024,128]{1,0:T(8,128)(2,1)} %ik_ref.1) | copy-start | bytes 786436
  5.5 0.7 copy-start.4
  6.2 0.7 copy-start.5

commit v2 on v1

v2 whole, which is shorter than its diff:
```python
import functools

import jax
import jax.numpy as jnp
from jax import lax
from jax.experimental import pallas as pl
from jax.experimental.pallas import tpu as pltpu
from jax.sharding import PartitionSpec as P

MESH = pl.DeviceIdType.MESH
F32 = jnp.float32
BF16 = jnp.bfloat16

Q, H, HI, DI = 64, 128, 64, 128
NZ = 8
NG = 8
HL = 32
JL = 16
KEYS = 1024
QB = 8
NB = Q // QB
CH = 32
LOG2E = 1.4426950408889634
SCORE_SCALE = (192 ** (-0.5)) * LOG2E
INDEX_SCALE = (HI * DI) ** (-0.5)
FILL = -1e30
LOSS_SCALE = 1024.0


def kernel(
    pos_ref, q_hbm, lat_hbm, iq_hbm, ik_hbm, wt_hbm,
    gq_ref, gk_ref,
    q_ref, lat_ref, iq_ref, ik_ref, wt_ref,
    prod_a, prod_b, mb, ex, iqf, iqp, iqt, ikt, dots, wpad, w_ref, coef,
    lg, lg_rc, lg_ry, lg_fin,
    tg, tg_rc, tg_ry, tg_fin,
    st, st_rz, st2, st_rx, fac,
    gq_tmp, gq, gq_rx, gz, gz_rx,
    gk_p, gk_rc, gk_s, gk_ry,
    load_sem, pair_send, pair_recv, send_z, recv_z, send_x, recv_x,
):
    c = lax.axis_index("ctx")
    h = lax.axis_index("heads")
    z, g = c % NZ, c // NZ
    core, ylo = h % 2, h // 2
    core_peer = (c, ylo * 2 + (1 - core))
    ylo_peer = (c, (1 - ylo) * 2 + core)
    far = (4, 3, 5, 2, 6, 1, 7)
    z_ids = [(z + k) % NZ for k in far]
    g_ids = [(g + k) % NG for k in far]
    z_peers = [(g * NZ + i, h) for i in z_ids]
    g_peers = [(i * NZ + z, h) for i in g_ids]
    peers = z_peers + g_peers + [core_peer, ylo_peer]

    def load(k, src, dst):
        copy = pltpu.make_async_copy(src, dst, load_sem.at[k])
        copy.start()
        return copy

    first_rows, last_rows = pl.ds(0, CH * HL), pl.ds(CH * HL, CH * HL)
    l_iq = load(0, iq_hbm, iq_ref)
    l_ik = load(1, ik_hbm, ik_ref)
    l_wt = load(2, wt_hbm, wt_ref)
    l_lat = load(3, lat_hbm, lat_ref)
    l_q0 = load(4, q_hbm.at[first_rows], q_ref.at[first_rows])
    l_q1 = load(5, q_hbm.at[last_rows], q_ref.at[last_rows])

    barrier = pltpu.get_barrier_semaphore()
    for p in peers:
        pl.semaphore_signal(barrier, inc=1, device_id=p, device_id_type=MESH)

    def remote(src, dst, send, recv, peer):
        return pltpu.make_async_remote_copy(
            src_ref=src, dst_ref=dst, send_sem=send, recv_sem=recv,
            device_id=peer, device_id_type=MESH,
        )

    def pair(slot, src, dst, peer):
        copy = remote(src, dst, pair_send.at[slot], pair_recv.at[slot], peer)
        copy.start()
        return copy

    def spread(slot, sends, recvs, targets, src, dst):
        copies = [
            remote(src(k), dst(k), sends.at[slot, k], recvs.at[slot, k], p)
            for k, p in enumerate(targets)
        ]
        for copy in copies:
            copy.start()
        return copies

    def wait(copies):
        for copy in copies:
            copy.wait()

    lane = lax.broadcasted_iota(jnp.int32, (QB, 128), 1)
    sub = lax.broadcasted_iota(jnp.int32, (QB, 128), 0)
    key_pos = c * KEYS + lane
    row_iota = lax.broadcasted_iota(jnp.int32, (QB, 1), 0)
    GROUPS = KEYS // 128

    def lanes(n):
        return slice(n * 128, (n + 1) * 128)

    def aligned(start, size, by=None):
        return pl.ds(pl.multiple_of(start, by or size), size)

    def tree(op, parts):
        parts = list(parts)
        while len(parts) > 1:
            parts = [op(*parts[i : i + 2]) if i + 1 < len(parts) else parts[i] for i in range(0, len(parts), 2)]
        return parts[0]

    l_iq.wait()
    iqf[...] = iq_ref[...].astype(F32)

    def permute(b, _):
        for j in range(0, JL, 2):
            two = [iqf[pl.ds(b * 128 + j + i, QB, stride=JL), :] for i in range(2)]
            iqp[aligned(b * 128 + j * QB, 2 * QB), :] = jnp.concatenate(two, axis=0).astype(BF16)
        return 0

    lax.fori_loop(0, NB, permute, 0)
    iqt[...] = iqp[...].T
    l_ik.wait()
    ikt[...] = ik_ref[...].T
    l_wt.wait()
    wpad[...] = jnp.zeros_like(wpad)
    wpad[0:JL, 0:Q] = wt_ref[...] * INDEX_SCALE
    w_ref[...] = wpad[...].T

    def index_block(b, _):
        rows = aligned(b * 128, 128)
        dots[rows, :] = jnp.dot(iqp[rows, :], ikt[...], preferred_element_type=F32)
        wb = w_ref[aligned(b * QB, QB), :]
        ws = [jnp.broadcast_to(wb[:, j : j + 1], (QB, 128)) for j in range(JL)]
        col = jnp.zeros((QB, 1), jnp.int32)
        for i in range(QB):
            col = jnp.where(row_iota == i, pos_ref[b * QB + i], col)
        col = jnp.broadcast_to(col, (QB, 128))
        for n in range(GROUPS):
            total = tree(jnp.add, [
                ws[j] * jnp.maximum(dots[aligned(b * 128 + j * QB, QB), lanes(n)], 0.0)
                for j in range(JL)
            ])
            lg[aligned(b * QB, QB), lanes(n)] = jnp.where(key_pos + n * 128 <= col, total, FILL)
        return 0

    lax.fori_loop(0, NB, index_block, 0)

    def multiply(b, prod):
        rows = aligned(b * (QB * HL), QB * HL)
        for n in range(KEYS // 256):
            at = slice(n * 256, (n + 1) * 256)
            prod[:, at] = jnp.dot(q_ref[rows, :], lat_ref[:, at], preferred_element_type=F32)

    def softmax(b, prod, carry):
        local = b % (CH // QB) * QB

        def peaks(k, ms):
            pos = pos_ref[b * QB + k]
            vis = [key_pos + n * 128 <= pos for n in range(GROUPS)]
            for i in range(HL // QB):
                rows = aligned(k * HL + i * QB, QB)
                m = tree(jnp.maximum, [
                    jnp.where(vis[n], prod[rows, lanes(n)], FILL) for n in range(GROUPS)
                ])
                m = jnp.broadcast_to(jnp.max(m, axis=1, keepdims=True) * SCORE_SCALE, (QB, 128))
                mb[rows, :] = m
                ms = jnp.where(lane == i * 32 + local + k, m, ms)
            return ms

        def masses(k, ls):
            pos = pos_ref[b * QB + k]
            vis = [key_pos + n * 128 <= pos for n in range(GROUPS)]
            for i in range(HL // QB):
                rows = aligned(k * HL + i * QB, QB)
                m = mb[rows, :]
                to = aligned(b * (QB * HL) + k * HL + i * QB, QB)
                es = []
                for n in range(GROUPS):
                    e = jnp.exp2(prod[rows, lanes(n)] * SCORE_SCALE - m)
                    e = jnp.where(vis[n], e, 0.0)
                    ex[to, lanes(n)] = e
                    es.append(e)
                l = jnp.sum(tree(jnp.add, es), axis=1, keepdims=True)
                ls = jnp.where(lane == i * 32 + local + k, l, ls)
            return ls

        ms = lax.fori_loop(0, QB, peaks, carry[0], unroll=True)
        ls = lax.fori_loop(0, QB, masses, carry[1], unroll=True)
        return ms, ls

    def two_blocks(i, carry):
        multiply(2 * i + 1, prod_b)
        carry = softmax(2 * i, prod_a, carry)
        multiply(jnp.minimum(2 * i + 2, NB - 1), prod_a)
        return softmax(2 * i + 1, prod_b, carry)

    def attention(first, last, carry):
        return lax.fori_loop(first, last, two_blocks, carry)

    zero = jnp.zeros((QB, 128), F32)
    half = aligned(core * 32, 32)
    other = aligned((1 - core) * 32, 32)

    l_lat.wait()
    l_q0.wait()
    multiply(0, prod_a)
    l_q1.wait()
    ms, ls = attention(0, 2, (zero, zero))
    st[0, 0:8, :] = ms
    st[0, 8:16, :] = ls
    pl.semaphore_wait(barrier, len(peers))
    s_z0 = spread(0, send_z, recv_z, z_peers, lambda k: st.at[0, 0:16], lambda k: st_rz.at[0, k, 0:16])
    copy = pair(0, lg.at[other], lg_rc, core_peer)
    carry = attention(2, 3, (zero, zero))
    copy.wait()
    lg[half, :] = lg[half, :] + lg_rc[...]
    copy = pair(1, lg.at[half], lg_ry, ylo_peer)
    ms, ls = attention(3, 4, carry)
    st[1, 0:8, :] = ms
    st[1, 8:16, :] = ls
    copy.wait()
    lg_fin[half, :] = lg[half, :] + lg_ry[...]
    copy = pair(2, lg_fin.at[half], lg_fin.at[half], core_peer)
    copy.wait()

    def index_stats(b, ix):
        rows = aligned(b * QB, QB)
        xs = [lg_fin[rows, lanes(n)] * LOG2E for n in range(GROUPS)]
        m = jnp.max(tree(jnp.maximum, xs), axis=1, keepdims=True)
        mm = jnp.broadcast_to(m, (QB, 128))
        l = jnp.sum(tree(jnp.add, [jnp.exp2(x - mm) for x in xs]), axis=1, keepdims=True)
        return jnp.where(lane == b, m, jnp.where(lane == b + 64, l, ix))

    st[1, 16:24, :] = lax.fori_loop(0, NB, index_stats, zero, unroll=True)
    s_z1 = spread(1, send_z, recv_z, z_peers, lambda k: st.at[1], lambda k: st_rz.at[1, k])

    def combine(own, received, with_index):
        parts = [own[...]] + [received[k] for k in range(7)]
        top = tree(jnp.maximum, [p[0:8] for p in parts])
        mass = tree(jnp.add, [p[8:16] * jnp.exp2(p[0:8] - top) for p in parts])
        if not with_index:
            return top, mass, None
        peak = tree(jnp.maximum, [p[16:24] for p in parts])
        low = lane < 64
        imass = tree(jnp.add, [
            p[16:24] * pltpu.roll(jnp.exp2(jnp.where(low, p[16:24] - peak, 0.0)), 64, 1)
            for p in parts
        ])
        return top, mass, jnp.where(low, peak, imass)

    def combined_z(t):
        top, mass, idx = combine(st.at[t], st_rz.at[t], t == 1)
        st2[t, 0:8, :] = top
        st2[t, 8:16, :] = mass
        if t == 0:
            return spread(
                t, send_x, recv_x, g_peers, lambda k: st2.at[0, 0:16], lambda k: st_rx.at[0, k, 0:16]
            )
        st2[t, 16:24, :] = idx
        return spread(t, send_x, recv_x, g_peers, lambda k: st2.at[1], lambda k: st_rx.at[1, k])

    def factors(t):
        top, mass, idx = combine(st2.at[t], st_rx.at[t], t == 1)
        fac[t] = jnp.exp2(st[t, 0:8, :] - top) / mass
        if t == 1:
            fac[2] = idx

    def turn(x, shift):
        return pltpu.roll(x, shift % QB, 0)

    def gathered(r):
        r = [r[i] for i in (3, 2, 1, 0, 7, 6, 5, 4)]
        low = sub < 4
        a = [
            jnp.where(low, r[i], r[i + 4]) + turn(jnp.where(low, r[i + 4], r[i]), 4)
            for i in range(4)
        ]
        low = sub % 4 < 2
        b = [jnp.where(low, a[i + 2] + turn(a[i + 2], -2), a[i] + turn(a[i], 2)) for i in range(2)]
        return jnp.where(sub % 2 < 1, b[1] + turn(b[1], -1), b[0] + turn(b[0], 1))

    def target(t):
        def block(b, _):
            f = pltpu.roll(fac[t], (128 - QB * b) % 128, 1)
            fs = [
                [jnp.broadcast_to(f[:, i * 32 + k : i * 32 + k + 1], (QB, 128)) for i in range(4)]
                for k in range(QB)
            ]
            for n in range(GROUPS):
                r = []
                for k in range(QB):
                    at = (t * (CH // QB) + b) * (QB * HL) + k * HL
                    r.append(tree(jnp.add, [
                        ex[aligned(at + i * QB, QB), lanes(n)] * fs[k][i] for i in range(4)
                    ]))
                tg[t, aligned(b * QB, QB), lanes(n)] = gathered(r)
            return 0

        lax.fori_loop(0, CH // QB, block, 0)

    part = aligned(core * 16, 16)
    other_part = aligned((1 - core) * 16, 16)

    def core_one(t):
        return pair(3 + t, tg.at[t, other_part], tg_rc.at[t], core_peer)

    def across(t):
        tg[t, part, :] = tg[t, part, :] + tg_rc[t]
        return pair(5 + t, tg.at[t, part], tg_ry.at[t], ylo_peer)

    def core_two(t):
        tg_fin[t, part, :] = tg[t, part, :] + tg_ry[t]
        return pair(7 + t, tg_fin.at[t, part], tg_fin.at[t, part], core_peer)

    def grads(t):
        def block(i, _):
            b = t * (CH // QB) + i
            rows = aligned(b * QB, QB)
            ix = fac[2]
            peak = jnp.sum(jnp.where(lane == b, ix, 0.0), axis=1, keepdims=True)
            mass = jnp.sum(jnp.where(lane == b + 64, ix, 0.0), axis=1, keepdims=True)
            peak = jnp.broadcast_to(peak, (QB, 128))
            share = jnp.broadcast_to(LOSS_SCALE / mass, (QB, 128))
            wb = w_ref[rows, :]
            ws = [jnp.broadcast_to(wb[:, j : j + 1], (QB, 128)) for j in range(JL)]
            for n in range(GROUPS):
                probs = jnp.exp2(lg_fin[rows, lanes(n)] * LOG2E - peak) * share
                grad = probs - tg_fin[t, aligned(i * QB, QB), lanes(n)] * (LOSS_SCALE / H)
                for j in range(0, JL, 2):
                    two = []
                    for jj in (j, j + 1):
                        d = dots[aligned(b * 128 + jj * QB, QB), lanes(n)]
                        two.append(jnp.where(d > 0.0, grad * ws[jj], 0.0))
                    at = aligned(b * 128 + j * QB, 2 * QB)
                    coef[at, lanes(n)] = jnp.concatenate(two, axis=0).astype(BF16)
            here = aligned(b * 128, 128)
            gq_tmp[...] = jnp.dot(coef[here, :], ik_ref[...], preferred_element_type=F32)
            for k in range(QB):
                gq[t, aligned(i * 128 + k * JL, JL), :] = gq_tmp[pl.ds(k, JL, stride=QB), :]
            return 0

        lax.fori_loop(0, CH // QB, block, 0)
        return spread(
            2 + t, send_x, recv_x, g_peers,
            lambda k: gq.at[t, aligned(g_ids[k] * 64, 64)], lambda k: gq_rx.at[t, k],
        )

    def sum_x(t):
        mine = gq[t, aligned(g * 64, 64), :]
        gz[t] = tree(jnp.add, [mine] + [gq_rx[t, k] for k in range(7)])
        gz_rx[t, z] = gz[t]
        return spread(
            2 + t, send_z, recv_z, z_peers, lambda k: gz.at[t], lambda k: gz_rx.at[t, z]
        )

    def sum_z(t):
        mine = aligned(t * 512 + g * 64, 64)
        gq_ref[mine, :] = tree(jnp.add, [gz_rx[t, k] for k in range(NZ)])
        return spread(
            4 + t, send_x, recv_x, g_peers, lambda k: gq_ref.at[mine], lambda k: gq_ref.at[mine]
        )

    wait(s_z0)
    s_x0 = combined_z(0)
    wait(s_z1)
    s_x1 = combined_z(1)
    wait(s_x0)
    factors(0)
    target(0)
    one0 = core_one(0)
    one0.wait()
    across0 = across(0)
    wait(s_x1)
    factors(1)
    target(1)
    one1 = core_one(1)
    across0.wait()
    two0 = core_two(0)
    one1.wait()
    across1 = across(1)
    two0.wait()
    rs0 = grads(0)
    across1.wait()
    two1 = core_two(1)
    two1.wait()
    rs1 = grads(1)

    for piece in range(4):
        gk_p[piece % 2, piece // 2] = jnp.dot(
            iqt[...], coef[:, piece * 256 : (piece + 1) * 256], preferred_element_type=F32
        )
    gk1 = pair(9, gk_p.at[1 - core], gk_rc, core_peer)
    wait(rs0)
    sz0 = sum_x(0)
    gk1.wait()
    gk_s[...] = gk_p[core] + gk_rc[...]
    gk2 = pair(10, gk_s.at[1 - ylo], gk_ry, ylo_peer)
    wait(rs1)
    sz1 = sum_x(1)
    gk2.wait()
    gk_ref[...] = (gk_s[ylo] + gk_ry[...]).T
    wait(sz0)
    ag0 = sum_z(0)
    wait(sz1)
    ag1 = sum_z(1)
    wait(ag0)
    wait(ag1)


def body(queries, latents, index_queries, index_keys, index_weights, positions):
    hbm = pl.BlockSpec(memory_space=pltpu.HBM)
    vmem = pl.BlockSpec(memory_space=pltpu.VMEM)
    smem = pl.BlockSpec(memory_space=pltpu.SMEM)
    rows = Q * HL
    v = pltpu.VMEM
    dma = pltpu.SemaphoreType.DMA
    scratch = [
        v((rows, queries.shape[2]), BF16),
        v((queries.shape[2], KEYS), BF16),
        v((Q * JL, DI), BF16),
        v((KEYS, DI), BF16),
        v((JL, Q), F32),
        v((QB * HL, KEYS), F32),
        v((QB * HL, KEYS), F32),
        v((QB * HL, 128), F32),
        v((rows, KEYS), F32),
        v((Q * JL, DI), F32),
        v((Q * JL, DI), BF16),
        v((DI, Q * JL), BF16),
        v((DI, KEYS), BF16),
        v((Q * JL, KEYS), F32),
        v((128, 128), F32),
        v((128, 128), F32),
        v((Q * JL, KEYS), BF16),
        v((Q, KEYS), F32), v((32, KEYS), F32), v((32, KEYS), F32), v((Q, KEYS), F32),
        v((2, CH, KEYS), F32), v((2, 16, KEYS), F32), v((2, 16, KEYS), F32), v((2, CH, KEYS), F32),
        v((2, 24, 128), F32), v((2, 7, 24, 128), F32),
        v((2, 24, 128), F32), v((2, 7, 24, 128), F32),
        v((3, 8, 128), F32),
        v((128, DI), F32), v((2, 512, DI), F32), v((2, 7, 64, DI), F32),
        v((2, 64, DI), F32), v((2, NZ, 64, DI), F32),
        v((2, 2, DI, 256), F32), v((2, DI, 256), F32), v((2, DI, 256), F32), v((DI, 256), F32),
        dma((6,)), dma((11,)), dma((11,)), dma((4, 7)), dma((4, 7)), dma((6, 7)), dma((6, 7)),
    ]
    grad_queries, grad_keys = pl.pallas_call(
        kernel,
        out_shape=(
            jax.ShapeDtypeStruct((Q * JL, DI), F32),
            jax.ShapeDtypeStruct((KEYS // 4, DI), F32),
        ),
        in_specs=[smem] + [hbm] * 5,
        out_specs=(vmem, vmem),
        scratch_shapes=scratch,
        compiler_params=pltpu.CompilerParams(
            collective_id=0, has_side_effects=True, vmem_limit_bytes=48 * 1024 * 1024
        ),
    )(
        positions,
        queries.reshape(rows, queries.shape[2]),
        latents.T,
        index_queries.reshape(Q * JL, DI),
        index_keys,
        index_weights.T,
    )
    return grad_queries.reshape(Q, JL, DI), grad_keys


def solution(mesh):
    placed = (
        P(None, "heads", None),
        P("ctx", None),
        P(None, "heads", None),
        P("ctx", None),
        P(None, "heads"),
        P(),
    )
    return jax.shard_map(
        body,
        mesh=mesh,
        in_specs=placed,
        out_specs=(P(None, "heads", None), P(("ctx", "heads"), None)),
        check_vma=False,
    )
```

time: 80.4 us -> 70.6 us (0.88)
  Pallas kernels: 71.8 us -> 61.7 us
    pallas_call x1, Pallas kernels: 71.8 us -> 61.7 us  [body(): pl.pallas_call(kernel, out_shape=(jax.ShapeDtypeStruct((Q * JL, DI), F32)...]
where the time goes in v2:
time: 70.6 us; the launch traced here: 70 us
  Pallas kernels  61.7 us (87%)
  local copies, waits for them, and re-layouts  7.7 us (11%)
    pallas_call x1, Pallas kernels, body(): pl.pallas_call(kernel, out_shape=(jax.ShapeDtypeStruct((Q * JL, DI), F32)...  61.7 us
    unnamed x14, local copies, waits for them, and re-layouts  7.7 us

profile of v2, /device:TPU:8, one launch (start us, length us, event | category | flops | bytes accessed | tf_op | source)
XLA Modules:
  0.0 70.0 jit_solution(4408267671574112075)
XLA Ops:
  0.6 0.0 copy-start
  0.6 1.7 %copy-done = bf16[64,32,576]{2,1,0:T(8,128)(2,1)S(1)} copy-done((bf16[64,32,576]{2,1,0:T(8,128)(2,1)S(1)}, bf16[64,32,576]{2,1,0:T(8,128)(2,1)}, u32[]{:S(2)}) %copy-start) | copy-done | bytes 2359320
  2.4 0.0 copy-start.1
  2.4 1.3 %copy-done.1 = bf16[1024,576]{0,1:T(8,128)(2,1)S(1)} copy-done((bf16[1024,576]{0,1:T(8,128)(2,1)S(1)}, bf16[1024,576]{0,1:T(8,128)(2,1)}, u32[]{:S(2)}) %copy-start.1) | copy-done | bytes 1179672
  3.6 0.0 copy-start.2
  3.6 0.9 %copy-done.2 = bf16[64,16,128]{2,1,0:T(8,128)(2,1)S(1)} copy-done((bf16[64,16,128]{2,1,0:T(8,128)(2,1)S(1)}, bf16[64,16,128]{2,1,0:T(8,128)(2,1)}, u32[]{:S(2)}) %copy-start.2) | copy-done | bytes 262168
  4.6 0.0 copy-start.3
  4.6 0.9 %copy-done.3 = bf16[1024,128]{1,0:T(8,128)(2,1)S(1)} copy-done((bf16[1024,128]{1,0:T(8,128)(2,1)S(1)}, bf16[1024,128]{1,0:T(8,128)(2,1)}, u32[]{:S(2)}) %copy-start.3) | copy-done | bytes 262168
  5.5 0.0 copy-start.4
  5.5 0.7 copy-done.4
  6.2 0.0 copy-start.5
  6.2 0.7 copy-done.5
  6.9 61.7 %shard_map.77 = (f32[1024,128]{1,0:T(8,128)S(1)}, f32[256,128]{1,0:T(8,128)S(1)}) custom-call(s32[64]{0:T(128)S(1)} %copy-done.5, bf16[2048,576]{1,0:T(8,128)(2,1)S(1)} %bitcast.5, bf16[576,1024]{1,0:T(8,128)(2,1)S(1)} %bitcast.6, bf16[1024,128]{1,0:T(8,128)(2,1)S(1)} %bitcast.8, bf16[1024,128]{1,0:T(8,128)(2,1)S(1)} %copy-done.3, f32[16,64]{1,0:T(8,128)S(1)} %bitcast.9), custom_call_target="tpu_custom_call" | custom-call | tf_op jit(solution)/shard_map/pallas_call | solution.py:448
  68.6 0.8 %copy.10 = f32[64,16,128]{2,1,0:T(8,128)} copy(f32[64,16,128]{2,1,0:T(8,128)S(1)} %bitcast.7) | data formatting | bytes 1048576
  69.4 0.7 copy.11
Async XLA Ops:
  0.6 1.7 %copy-start = (bf16[64,32,576]{2,1,0:T(8,128)(2,1)S(1)}, bf16[64,32,576]{2,1,0:T(8,128)(2,1)}, u32[]{:S(2)}) copy-start(bf16[64,32,576]{2,1,0:T(8,128)(2,1)} %param.6) | copy-start | bytes 7077892
  2.4 1.3 %copy-start.1 = (bf16[1024,576]{0,1:T(8,128)(2,1)S(1)}, bf16[1024,576]{0,1:T(8,128)(2,1)}, u32[]{:S(2)}) copy-start(bf16[1024,576]{0,1:T(8,128)(2,1)} %param.7) | copy-start | bytes 3538948
  3.6 0.9 %copy-start.2 = (bf16[64,16,128]{2,1,0:T(8,128)(2,1)S(1)}, bf16[64,16,128]{2,1,0:T(8,128)(2,1)}, u32[]{:S(2)}) copy-start(bf16[64,16,128]{2,1,0:T(8,128)(2,1)} %param.8) | copy-start | bytes 786436
  4.6 0.9 %copy-start.3 = (bf16[1024,128]{1,0:T(8,128)(2,1)S(1)}, bf16[1024,128]{1,0:T(8,128)(2,1)}, u32[]{:S(2)}) copy-start(bf16[1024,128]{1,0:T(8,128)(2,1)} %ik_hbm.1) | copy-start | bytes 786436
  5.5 0.7 copy-start.4
  6.2 0.7 copy-start.5

commit v3 on v2

--- a/solution.py
+++ b/solution.py
@@ -34,9 +34,9 @@
     prod_a, prod_b, mb, ex, iqf, iqp, iqt, ikt, dots, wpad, w_ref, coef,
     lg, lg_rc, lg_ry, lg_fin,
     tg, tg_rc, tg_ry, tg_fin,
-    st, st_rz, st2, st_rx, fac,
+    st, st_rz, st2, st_rx, ix, ix_rz, ix2, ix_rx, fac,
     gq_tmp, gq, gq_rx, gz, gz_rx,
-    gk_p, gk_rc, gk_s, gk_ry,
+    gk_p, gk_rc, gk_s, gk_ry, gsum, gk_out,
     load_sem, pair_send, pair_recv, send_z, recv_z, send_x, recv_x,
 ):
     c = lax.axis_index("ctx")
@@ -129,9 +129,11 @@
     wpad[0:JL, 0:Q] = wt_ref[...] * INDEX_SCALE
     w_ref[...] = wpad[...].T
 
+    for n in range(KEYS // 256):
+        at = slice(n * 256, (n + 1) * 256)
+        dots[:, at] = jnp.dot(iqp[...], ikt[:, at], preferred_element_type=F32)
+
     def index_block(b, _):
-        rows = aligned(b * 128, 128)
-        dots[rows, :] = jnp.dot(iqp[rows, :], ikt[...], preferred_element_type=F32)
         wb = w_ref[aligned(b * QB, QB), :]
         ws = [jnp.broadcast_to(wb[:, j : j + 1], (QB, 128)) for j in range(JL)]
         col = jnp.zeros((QB, 1), jnp.int32)
@@ -146,7 +148,7 @@
             lg[aligned(b * QB, QB), lanes(n)] = jnp.where(key_pos + n * 128 <= col, total, FILL)
         return 0
 
-    lax.fori_loop(0, NB, index_block, 0)
+    lax.fori_loop(0, NB, index_block, 0, unroll=True)
 
     def multiply(b, prod):
         rows = aligned(b * (QB * HL), QB * HL)
@@ -212,61 +214,49 @@
     st[0, 0:8, :] = ms
     st[0, 8:16, :] = ls
     pl.semaphore_wait(barrier, len(peers))
-    s_z0 = spread(0, send_z, recv_z, z_peers, lambda k: st.at[0, 0:16], lambda k: st_rz.at[0, k, 0:16])
-    copy = pair(0, lg.at[other], lg_rc, core_peer)
+    s_z0 = spread(0, send_z, recv_z, z_peers, lambda k: st.at[0], lambda k: st_rz.at[0, k])
+    lg1 = pair(0, lg.at[other], lg_rc, core_peer)
     carry = attention(2, 3, (zero, zero))
-    copy.wait()
+    lg1.wait()
     lg[half, :] = lg[half, :] + lg_rc[...]
-    copy = pair(1, lg.at[half], lg_ry, ylo_peer)
+    lg2 = pair(1, lg.at[half], lg_ry, ylo_peer)
     ms, ls = attention(3, 4, carry)
     st[1, 0:8, :] = ms
     st[1, 8:16, :] = ls
-    copy.wait()
-    lg_fin[half, :] = lg[half, :] + lg_ry[...]
-    copy = pair(2, lg_fin.at[half], lg_fin.at[half], core_peer)
-    copy.wait()
-
-    def index_stats(b, ix):
+    s_z1 = spread(1, send_z, recv_z, z_peers, lambda k: st.at[1], lambda k: st_rz.at[1, k])
+
+    def index_stats(b, so_far):
         rows = aligned(b * QB, QB)
         xs = [lg_fin[rows, lanes(n)] * LOG2E for n in range(GROUPS)]
         m = jnp.max(tree(jnp.maximum, xs), axis=1, keepdims=True)
         mm = jnp.broadcast_to(m, (QB, 128))
         l = jnp.sum(tree(jnp.add, [jnp.exp2(x - mm) for x in xs]), axis=1, keepdims=True)
-        return jnp.where(lane == b, m, jnp.where(lane == b + 64, l, ix))
-
-    st[1, 16:24, :] = lax.fori_loop(0, NB, index_stats, zero, unroll=True)
-    s_z1 = spread(1, send_z, recv_z, z_peers, lambda k: st.at[1], lambda k: st_rz.at[1, k])
-
-    def combine(own, received, with_index):
+        return jnp.where(lane == b, m, jnp.where(lane == b + 64, l, so_far))
+
+    def combine(own, received):
         parts = [own[...]] + [received[k] for k in range(7)]
         top = tree(jnp.maximum, [p[0:8] for p in parts])
         mass = tree(jnp.add, [p[8:16] * jnp.exp2(p[0:8] - top) for p in parts])
-        if not with_index:
-            return top, mass, None
-        peak = tree(jnp.maximum, [p[16:24] for p in parts])
+        return top, mass
+
+    def combine_index(own, received):
+        parts = [own[...]] + [received[k] for k in range(7)]
+        peak = tree(jnp.maximum, parts)
         low = lane < 64
-        imass = tree(jnp.add, [
-            p[16:24] * pltpu.roll(jnp.exp2(jnp.where(low, p[16:24] - peak, 0.0)), 64, 1)
-            for p in parts
+        mass = tree(jnp.add, [
+            p * pltpu.roll(jnp.exp2(jnp.where(low, p - peak, 0.0)), 64, 1) for p in parts
         ])
-        return top, mass, jnp.where(low, peak, imass)
+        return jnp.where(low, peak, mass)
 
     def combined_z(t):
-        top, mass, idx = combine(st.at[t], st_rz.at[t], t == 1)
+        top, mass = combine(st.at[t], st_rz.at[t])
         st2[t, 0:8, :] = top
         st2[t, 8:16, :] = mass
-        if t == 0:
-            return spread(
-                t, send_x, recv_x, g_peers, lambda k: st2.at[0, 0:16], lambda k: st_rx.at[0, k, 0:16]
-            )
-        st2[t, 16:24, :] = idx
-        return spread(t, send_x, recv_x, g_peers, lambda k: st2.at[1], lambda k: st_rx.at[1, k])
+        return spread(t, send_x, recv_x, g_peers, lambda k: st2.at[t], lambda k: st_rx.at[t, k])
 
     def factors(t):
-        top, mass, idx = combine(st2.at[t], st_rx.at[t], t == 1)
+        top, mass = combine(st2.at[t], st_rx.at[t])
         fac[t] = jnp.exp2(st[t, 0:8, :] - top) / mass
-        if t == 1:
-            fac[2] = idx
 
     def turn(x, shift):
         return pltpu.roll(x, shift % QB, 0)
@@ -283,10 +273,13 @@
         return jnp.where(sub % 2 < 1, b[1] + turn(b[1], -1), b[0] + turn(b[0], 1))
 
     def target(t):
-        def block(b, _):
-            f = pltpu.roll(fac[t], (128 - QB * b) % 128, 1)
+        f = fac[t]
+        for b in range(CH // QB):
             fs = [
-                [jnp.broadcast_to(f[:, i * 32 + k : i * 32 + k + 1], (QB, 128)) for i in range(4)]
+                [
+                    jnp.broadcast_to(f[:, i * 32 + b * QB + k : i * 32 + b * QB + k + 1], (QB, 128))
+                    for i in range(4)
+                ]
                 for k in range(QB)
             ]
             for n in range(GROUPS):
@@ -294,12 +287,9 @@
                 for k in range(QB):
                     at = (t * (CH // QB) + b) * (QB * HL) + k * HL
                     r.append(tree(jnp.add, [
-                        ex[aligned(at + i * QB, QB), lanes(n)] * fs[k][i] for i in range(4)
+                        ex[at + i * QB : at + (i + 1) * QB, lanes(n)] * fs[k][i] for i in range(4)
                     ]))
-                tg[t, aligned(b * QB, QB), lanes(n)] = gathered(r)
-            return 0
-
-        lax.fori_loop(0, CH // QB, block, 0)
+                tg[t, b * QB : (b + 1) * QB, lanes(n)] = gathered(r)
 
     part = aligned(core * 16, 16)
     other_part = aligned((1 - core) * 16, 16)
@@ -316,33 +306,32 @@
         return pair(7 + t, tg_fin.at[t, part], tg_fin.at[t, part], core_peer)
 
     def grads(t):
-        def block(i, _):
+        totals = fac[2]
+        for i in range(CH // QB):
             b = t * (CH // QB) + i
-            rows = aligned(b * QB, QB)
-            ix = fac[2]
-            peak = jnp.sum(jnp.where(lane == b, ix, 0.0), axis=1, keepdims=True)
-            mass = jnp.sum(jnp.where(lane == b + 64, ix, 0.0), axis=1, keepdims=True)
-            peak = jnp.broadcast_to(peak, (QB, 128))
-            share = jnp.broadcast_to(LOSS_SCALE / mass, (QB, 128))
+            rows = slice(b * QB, (b + 1) * QB)
+            peak = jnp.broadcast_to(totals[:, b : b + 1], (QB, 128))
+            share = jnp.broadcast_to(LOSS_SCALE / totals[:, b + 64 : b + 65], (QB, 128))
             wb = w_ref[rows, :]
             ws = [jnp.broadcast_to(wb[:, j : j + 1], (QB, 128)) for j in range(JL)]
             for n in range(GROUPS):
                 probs = jnp.exp2(lg_fin[rows, lanes(n)] * LOG2E - peak) * share
-                grad = probs - tg_fin[t, aligned(i * QB, QB), lanes(n)] * (LOSS_SCALE / H)
+                grad = probs - tg_fin[t, i * QB : (i + 1) * QB, lanes(n)] * (LOSS_SCALE / H)
                 for j in range(0, JL, 2):
                     two = []
                     for jj in (j, j + 1):
-                        d = dots[aligned(b * 128 + jj * QB, QB), lanes(n)]
+                        d = dots[b * 128 + jj * QB : b * 128 + (jj + 1) * QB, lanes(n)]
                         two.append(jnp.where(d > 0.0, grad * ws[jj], 0.0))
-                    at = aligned(b * 128 + j * QB, 2 * QB)
+                    at = slice(b * 128 + j * QB, b * 128 + (j + 2) * QB)
                     coef[at, lanes(n)] = jnp.concatenate(two, axis=0).astype(BF16)
-            here = aligned(b * 128, 128)
-            gq_tmp[...] = jnp.dot(coef[here, :], ik_ref[...], preferred_element_type=F32)
+        gq_tmp[...] = jnp.dot(
+            coef[t * 512 : (t + 1) * 512, :], ik_ref[...], preferred_element_type=F32
+        )
+        for i in range(CH // QB):
             for k in range(QB):
-                gq[t, aligned(i * 128 + k * JL, JL), :] = gq_tmp[pl.ds(k, JL, stride=QB), :]
-            return 0
-
-        lax.fori_loop(0, CH // QB, block, 0)
+                gq[t, i * 128 + k * JL : i * 128 + (k + 1) * JL, :] = gq_tmp[
+                    pl.ds(i * 128 + k, JL, stride=QB), :
+                ]
         return spread(
             2 + t, send_x, recv_x, g_peers,
             lambda k: gq.at[t, aligned(g_ids[k] * 64, 64)], lambda k: gq_rx.at[t, k],
@@ -358,19 +347,29 @@
 
     def sum_z(t):
         mine = aligned(t * 512 + g * 64, 64)
-        gq_ref[mine, :] = tree(jnp.add, [gz_rx[t, k] for k in range(NZ)])
-        return spread(
-            4 + t, send_x, recv_x, g_peers, lambda k: gq_ref.at[mine], lambda k: gq_ref.at[mine]
-        )
+        gsum[t] = tree(jnp.add, [gz_rx[t, k] for k in range(NZ)])
+        copies = spread(
+            4 + t, send_x, recv_x, g_peers, lambda k: gsum.at[t], lambda k: gq_ref.at[mine]
+        )
+        return copies + [load(t, gsum.at[t], gq_ref.at[mine])]
 
     wait(s_z0)
     s_x0 = combined_z(0)
+    lg2.wait()
+    lg_fin[half, :] = lg[half, :] + lg_ry[...]
+    lg3 = pair(2, lg_fin.at[half], lg_fin.at[half], core_peer)
+    lg3.wait()
+    ix[...] = lax.fori_loop(0, NB, index_stats, zero, unroll=True)
+    i_z = spread(4, send_z, recv_z, z_peers, lambda k: ix, lambda k: ix_rz.at[k])
     wait(s_z1)
     s_x1 = combined_z(1)
     wait(s_x0)
     factors(0)
     target(0)
     one0 = core_one(0)
+    wait(i_z)
+    ix2[...] = combine_index(ix, ix_rz)
+    i_x = spread(6, send_x, recv_x, g_peers, lambda k: ix2, lambda k: ix_rx.at[k])
     one0.wait()
     across0 = across(0)
     wait(s_x1)
@@ -381,6 +380,8 @@
     two0 = core_two(0)
     one1.wait()
     across1 = across(1)
+    wait(i_x)
+    fac[2] = combine_index(ix2, ix_rx)
     two0.wait()
     rs0 = grads(0)
     across1.wait()
@@ -401,18 +402,19 @@
     wait(rs1)
     sz1 = sum_x(1)
     gk2.wait()
-    gk_ref[...] = (gk_s[ylo] + gk_ry[...]).T
+    gk_out[...] = (gk_s[ylo] + gk_ry[...]).T
+    gk_store = load(2, gk_out, gk_ref)
     wait(sz0)
     ag0 = sum_z(0)
     wait(sz1)
     ag1 = sum_z(1)
     wait(ag0)
     wait(ag1)
+    gk_store.wait()
 
 
 def body(queries, latents, index_queries, index_keys, index_weights, positions):
     hbm = pl.BlockSpec(memory_space=pltpu.HBM)
-    vmem = pl.BlockSpec(memory_space=pltpu.VMEM)
     smem = pl.BlockSpec(memory_space=pltpu.SMEM)
     rows = Q * HL
     v = pltpu.VMEM
@@ -437,13 +439,15 @@
         v((Q * JL, KEYS), BF16),
         v((Q, KEYS), F32), v((32, KEYS), F32), v((32, KEYS), F32), v((Q, KEYS), F32),
         v((2, CH, KEYS), F32), v((2, 16, KEYS), F32), v((2, 16, KEYS), F32), v((2, CH, KEYS), F32),
-        v((2, 24, 128), F32), v((2, 7, 24, 128), F32),
-        v((2, 24, 128), F32), v((2, 7, 24, 128), F32),
+        v((2, 16, 128), F32), v((2, 7, 16, 128), F32),
+        v((2, 16, 128), F32), v((2, 7, 16, 128), F32),
+        v((8, 128), F32), v((7, 8, 128), F32), v((8, 128), F32), v((7, 8, 128), F32),
         v((3, 8, 128), F32),
-        v((128, DI), F32), v((2, 512, DI), F32), v((2, 7, 64, DI), F32),
+        v((512, DI), F32), v((2, 512, DI), F32), v((2, 7, 64, DI), F32),
         v((2, 64, DI), F32), v((2, NZ, 64, DI), F32),
         v((2, 2, DI, 256), F32), v((2, DI, 256), F32), v((2, DI, 256), F32), v((DI, 256), F32),
-        dma((6,)), dma((11,)), dma((11,)), dma((4, 7)), dma((4, 7)), dma((6, 7)), dma((6, 7)),
+        v((2, 64, DI), F32), v((KEYS // 4, DI), F32),
+        dma((6,)), dma((11,)), dma((11,)), dma((5, 7)), dma((5, 7)), dma((7, 7)), dma((7, 7)),
     ]
     grad_queries, grad_keys = pl.pallas_call(
         kernel,
@@ -452,10 +456,10 @@
             jax.ShapeDtypeStruct((KEYS // 4, DI), F32),
         ),
         in_specs=[smem] + [hbm] * 5,
-        out_specs=(vmem, vmem),
+        out_specs=(hbm, hbm),
         scratch_shapes=scratch,
         compiler_params=pltpu.CompilerParams(
-            collective_id=0, has_side_effects=True, vmem_limit_bytes=48 * 1024 * 1024
+            collective_id=0, has_side_effects=True, vmem_limit_bytes=63 * 1024 * 1024
         ),
     )(
         positions,

time: 70.6 us -> 60.5 us (0.86)
  Pallas kernels: 61.7 us -> 56 us
  local copies, waits for them, and re-layouts: 7.7 us -> 3.44 us
    pallas_call x1, Pallas kernels: 61.7 us -> 56 us  [body(): pl.pallas_call(kernel, out_shape=(jax.ShapeDtypeStruct((Q * JL, DI), F32)...]
    unnamed x14 -> x2, local copies, waits for them, and re-layouts: 7.7 us -> 3.44 us
where the time goes in v3:
time: 60.5 us; the launch traced here: 60 us
  Pallas kernels  56 us (93%)
  local copies, waits for them, and re-layouts  3.44 us (6%)
  between operations  0.64 us (1%)
    pallas_call x1, Pallas kernels, body(): pl.pallas_call(kernel, out_shape=(jax.ShapeDtypeStruct((Q * JL, DI), F32)...  56 us
    unnamed x2, local copies, waits for them, and re-layouts  3.44 us

profile of v3, /device:TPU:8, one launch (start us, length us, event | category | flops | bytes accessed | tf_op | source)
XLA Modules:
  0.0 60.0 jit_solution(8829030685572683527)
XLA Ops:
  0.6 56.0 %shard_map.77 = (f32[1024,128]{1,0:T(8,128)}, f32[256,128]{1,0:T(8,128)}) custom-call(s32[64]{0:T(128)} %pos_ref.1, bf16[2048,576]{1,0:T(8,128)(2,1)} %bitcast.5, bf16[576,1024]{1,0:T(8,128)(2,1)} %bitcast.6, bf16[1024,128]{1,0:T(8,128)(2,1)} %bitcast.8, bf16[1024,128]{1,0:T(8,128)(2,1)} %ik_hbm.1, f32[16,64]{1,0:T(8,128)} %bitcast.9), custom_call_target="tpu_custom_call" | custom-call | tf_op jit(solution)/shard_map/pallas_call | solution.py:452
  56.6 1.9 %copy.10 = f32[64,16,128]{2,1,0:T(8,128)} copy(f32[64,16,128]{2,1,0:T(8,128)} %bitcast.7) | data formatting | bytes 1048576
  58.5 1.6 %copy.11 = f32[256,128]{1,0:T(8,128)} copy(f32[256,128]{1,0:T(8,128)} %get-tuple-element.9) | data formatting | bytes 262144

commit v4 on v3

--- a/solution.py
+++ b/solution.py
@@ -52,6 +52,10 @@
     g_peers = [(i * NZ + z, h) for i in g_ids]
     peers = z_peers + g_peers + [core_peer, ylo_peer]
 
+    barrier = pltpu.get_barrier_semaphore()
+    for p in peers:
+        pl.semaphore_signal(barrier, inc=1, device_id=p, device_id_type=MESH)
+
     def load(k, src, dst):
         copy = pltpu.make_async_copy(src, dst, load_sem.at[k])
         copy.start()
@@ -64,10 +68,6 @@
     l_lat = load(3, lat_hbm, lat_ref)
     l_q0 = load(4, q_hbm.at[first_rows], q_ref.at[first_rows])
     l_q1 = load(5, q_hbm.at[last_rows], q_ref.at[last_rows])
-
-    barrier = pltpu.get_barrier_semaphore()
-    for p in peers:
-        pl.semaphore_signal(barrier, inc=1, device_id=p, device_id_type=MESH)
 
     def remote(src, dst, send, recv, peer):
         return pltpu.make_async_remote_copy(
@@ -411,6 +411,26 @@
     wait(ag0)
     wait(ag1)
     gk_store.wait()
+
+
+def deliver(gq_in, gk_in, gq_out, gk_out, gq_buf, gk_buf, arrive, leave):
+    part = Q * JL // 4
+
+    def piece(k):
+        return pl.ds(k * part, part)
+
+    first = [pltpu.make_async_copy(gk_in, gk_buf, arrive.at[4])]
+    last = [pltpu.make_async_copy(gk_buf, gk_out, leave.at[4])]
+    for k in range(4):
+        first.append(pltpu.make_async_copy(gq_in.at[piece(k)], gq_buf.at[piece(k)], arrive.at[k]))
+        last.append(pltpu.make_async_copy(gq_buf.at[piece(k)], gq_out.at[piece(k)], leave.at[k]))
+    for copy in first:
+        copy.start()
+    for one, two in zip(first, last):
+        one.wait()
+        two.start()
+    for copy in last:
+        copy.wait()
 
 
 def body(queries, latents, index_queries, index_keys, index_weights, positions):
@@ -469,6 +489,17 @@
         index_keys,
         index_weights.T,
     )
+    grad_queries, grad_keys = pl.pallas_call(
+        deliver,
+        out_shape=(
+            jax.ShapeDtypeStruct((Q * JL, DI), F32),
+            jax.ShapeDtypeStruct((KEYS // 4, DI), F32),
+        ),
+        in_specs=[hbm, hbm],
+        out_specs=(hbm, hbm),
+        scratch_shapes=[v((Q * JL, DI), F32), v((KEYS // 4, DI), F32), dma((5,)), dma((5,))],
+        compiler_params=pltpu.CompilerParams(vmem_limit_bytes=63 * 1024 * 1024),
+    )(grad_queries, grad_keys)
     return grad_queries.reshape(Q, JL, DI), grad_keys
 
 

time: 60.5 us -> 59.1 us (0.977)
  local copies, waits for them, and re-layouts: 3.44 us -> 0 us
  Pallas kernels: 56 us -> 58.1 us
    unnamed x2 -> x0, local copies, waits for them, and re-layouts: 3.44 us -> none
    pallas_call x0 -> x1, Pallas kernels: none -> 1.91 us  [body(): pl.pallas_call(deliver, out_shape=(jax.ShapeDtypeStruct((Q * JL, DI), F32...]
where the time goes in v4:
time: 59.1 us; the launch traced here: 58.7 us
  Pallas kernels  58.1 us (98%)
  between operations  0.64 us (1%)
    pallas_call x1, Pallas kernels, body(): pl.pallas_call(kernel, out_shape=(jax.ShapeDtypeStruct((Q * JL, DI), F32)...  56.2 us
    pallas_call x1, Pallas kernels, body(): pl.pallas_call(deliver, out_shape=(jax.ShapeDtypeStruct((Q * JL, DI), F32...  1.91 us

profile of v4, /device:TPU:8, one launch (start us, length us, event | category | flops | bytes accessed | tf_op | source)
XLA Modules:
  0.0 58.7 jit_solution(11034326862008699876)
XLA Ops:
  0.6 56.2 %shard_map.77 = (f32[1024,128]{1,0:T(8,128)}, f32[256,128]{1,0:T(8,128)}) custom-call(s32[64]{0:T(128)} %pos_ref.1, bf16[2048,576]{1,0:T(8,128)(2,1)} %bitcast.5, bf16[576,1024]{1,0:T(8,128)(2,1)} %bitcast.6, bf16[1024,128]{1,0:T(8,128)(2,1)} %bitcast.7, bf16[1024,128]{1,0:T(8,128)(2,1)} %ik_hbm.1, f32[16,64]{1,0:T(8,128)} %bitcast.8), custom_call_target="tpu_custom_call" | custom-call | tf_op jit(solution)/shard_map/pallas_call | solution.py:472
  56.8 1.9 %shard_map.78 = (f32[1024,128]{1,0:T(8,128)}, f32[256,128]{1,0:T(8,128)}) custom-call(f32[1024,128]{1,0:T(8,128)} %get-tuple-element.6.gq_in, f32[256,128]{1,0:T(8,128)} %get-tuple-element.7.gk_in), custom_call_target="tpu_custom_call" | custom-call | tf_op jit(solution)/shard_map/pallas_call | solution.py:492

commit v5 on v4

--- a/solution.py
+++ b/solution.py
@@ -210,20 +210,17 @@
     l_q0.wait()
     multiply(0, prod_a)
     l_q1.wait()
-    ms, ls = attention(0, 2, (zero, zero))
-    st[0, 0:8, :] = ms
-    st[0, 8:16, :] = ls
+    for t in range(2):
+        ms, ls = attention(2 * t, 2 * t + 2, (zero, zero))
+        st[t, 0:8, :] = ms
+        st[t, 8:16, :] = ls
     pl.semaphore_wait(barrier, len(peers))
     s_z0 = spread(0, send_z, recv_z, z_peers, lambda k: st.at[0], lambda k: st_rz.at[0, k])
     lg1 = pair(0, lg.at[other], lg_rc, core_peer)
-    carry = attention(2, 3, (zero, zero))
+    s_z1 = spread(1, send_z, recv_z, z_peers, lambda k: st.at[1], lambda k: st_rz.at[1, k])
     lg1.wait()
     lg[half, :] = lg[half, :] + lg_rc[...]
     lg2 = pair(1, lg.at[half], lg_ry, ylo_peer)
-    ms, ls = attention(3, 4, carry)
-    st[1, 0:8, :] = ms
-    st[1, 8:16, :] = ls
-    s_z1 = spread(1, send_z, recv_z, z_peers, lambda k: st.at[1], lambda k: st_rz.at[1, k])
 
     def index_stats(b, so_far):
         rows = aligned(b * QB, QB)

time: 59.1 us -> 61.7 us (1.044)
  Pallas kernels: 58.1 us -> 60.9 us
    pallas_call x1, Pallas kernels: 56.2 us -> 59 us  [body(): pl.pallas_call(kernel, out_shape=(jax.ShapeDtypeStruct((Q * JL, DI), F32)...]
where the time goes in v5:
time: 61.7 us; the launch traced here: 61.5 us
  Pallas kernels  60.9 us (99%)
  between operations  0.64 us (1%)
    pallas_call x1, Pallas kernels, body(): pl.pallas_call(kernel, out_shape=(jax.ShapeDtypeStruct((Q * JL, DI), F32)...  59 us
    pallas_call x1, Pallas kernels, body(): pl.pallas_call(deliver, out_shape=(jax.ShapeDtypeStruct((Q * JL, DI), F32...  1.91 us

profile of v5, /device:TPU:8, one launch (start us, length us, event | category | flops | bytes accessed | tf_op | source)
XLA Modules:
  0.0 61.5 jit_solution(10088372976704337576)
XLA Ops:
  0.6 59.0 %shard_map.77 = (f32[1024,128]{1,0:T(8,128)}, f32[256,128]{1,0:T(8,128)}) custom-call(s32[64]{0:T(128)} %pos_ref.1, bf16[2048,576]{1,0:T(8,128)(2,1)} %bitcast.5, bf16[576,1024]{1,0:T(8,128)(2,1)} %bitcast.6, bf16[1024,128]{1,0:T(8,128)(2,1)} %bitcast.7, bf16[1024,128]{1,0:T(8,128)(2,1)} %ik_hbm.1, f32[16,64]{1,0:T(8,128)} %bitcast.8), custom_call_target="tpu_custom_call" | custom-call | tf_op jit(solution)/shard_map/pallas_call | solution.py:469
  59.6 1.9 %shard_map.78 = (f32[1024,128]{1,0:T(8,128)}, f32[256,128]{1,0:T(8,128)}) custom-call(f32[1024,128]{1,0:T(8,128)} %get-tuple-element.6.gq_in, f32[256,128]{1,0:T(8,128)} %get-tuple-element.7.gk_in), custom_call_target="tpu_custom_call" | custom-call | tf_op jit(solution)/shard_map/pallas_call | solution.py:489

commit v6 on v4

--- a/solution.py
+++ b/solution.py
@@ -33,7 +33,7 @@
     q_ref, lat_ref, iq_ref, ik_ref, wt_ref,
     prod_a, prod_b, mb, ex, iqf, iqp, iqt, ikt, dots, wpad, w_ref, coef,
     lg, lg_rc, lg_ry, lg_fin,
-    tg, tg_rc, tg_ry, tg_fin,
+    tg, tg_rc, tg_ry, tg_co, tg_fin,
     st, st_rz, st2, st_rx, ix, ix_rz, ix2, ix_rx, fac,
     gq_tmp, gq, gq_rx, gz, gz_rx,
     gk_p, gk_rc, gk_s, gk_ry, gsum, gk_out,
@@ -45,12 +45,13 @@
     core, ylo = h % 2, h // 2
     core_peer = (c, ylo * 2 + (1 - core))
     ylo_peer = (c, (1 - ylo) * 2 + core)
+    cross_peer = (c, (1 - ylo) * 2 + (1 - core))
     far = (4, 3, 5, 2, 6, 1, 7)
     z_ids = [(z + k) % NZ for k in far]
     g_ids = [(g + k) % NG for k in far]
     z_peers = [(g * NZ + i, h) for i in z_ids]
     g_peers = [(i * NZ + z, h) for i in g_ids]
-    peers = z_peers + g_peers + [core_peer, ylo_peer]
+    peers = z_peers + g_peers + [core_peer, ylo_peer, cross_peer]
 
     barrier = pltpu.get_barrier_semaphore()
     for p in peers:
@@ -299,11 +300,17 @@
 
     def across(t):
         tg[t, part, :] = tg[t, part, :] + tg_rc[t]
-        return pair(5 + t, tg.at[t, part], tg_ry.at[t], ylo_peer)
-
-    def core_two(t):
-        tg_fin[t, part, :] = tg[t, part, :] + tg_ry[t]
-        return pair(7 + t, tg_fin.at[t, part], tg_fin.at[t, part], core_peer)
+        mine = tg.at[t, part]
+        return [
+            pair(5 + t, mine, tg_ry.at[t, part], ylo_peer),
+            pair(7 + t, mine, tg_ry.at[t, part], cross_peer),
+            pair(11 + t, mine, tg_co.at[t], core_peer),
+        ]
+
+    def complete(t, copies):
+        wait(copies)
+        tg_fin[t, part, :] = tg[t, part, :] + tg_ry[t, part, :]
+        tg_fin[t, other_part, :] = tg_co[t] + tg_ry[t, other_part, :]
 
     def grads(t):
         totals = fac[2]
@@ -353,11 +360,11 @@
         )
         return copies + [load(t, gsum.at[t], gq_ref.at[mine])]
 
-    wait(s_z0)
-    s_x0 = combined_z(0)
     lg2.wait()
     lg_fin[half, :] = lg[half, :] + lg_ry[...]
     lg3 = pair(2, lg_fin.at[half], lg_fin.at[half], core_peer)
+    wait(s_z0)
+    s_x0 = combined_z(0)
     lg3.wait()
     ix[...] = lax.fori_loop(0, NB, index_stats, zero, unroll=True)
     i_z = spread(4, send_z, recv_z, z_peers, lambda k: ix, lambda k: ix_rz.at[k])
@@ -376,17 +383,13 @@
     factors(1)
     target(1)
     one1 = core_one(1)
-    across0.wait()
-    two0 = core_two(0)
     one1.wait()
     across1 = across(1)
+    complete(0, across0)
     wait(i_x)
     fac[2] = combine_index(ix2, ix_rx)
-    two0.wait()
     rs0 = grads(0)
-    across1.wait()
-    two1 = core_two(1)
-    two1.wait()
+    complete(1, across1)
     rs1 = grads(1)
 
     for piece in range(4):
@@ -458,7 +461,8 @@
         v((128, 128), F32),
         v((Q * JL, KEYS), BF16),
         v((Q, KEYS), F32), v((32, KEYS), F32), v((32, KEYS), F32), v((Q, KEYS), F32),
-        v((2, CH, KEYS), F32), v((2, 16, KEYS), F32), v((2, 16, KEYS), F32), v((2, CH, KEYS), F32),
+        v((2, CH, KEYS), F32), v((2, 16, KEYS), F32), v((2, CH, KEYS), F32),
+        v((2, 16, KEYS), F32), v((2, CH, KEYS), F32),
         v((2, 16, 128), F32), v((2, 7, 16, 128), F32),
         v((2, 16, 128), F32), v((2, 7, 16, 128), F32),
         v((8, 128), F32), v((7, 8, 128), F32), v((8, 128), F32), v((7, 8, 128), F32),
@@ -467,7 +471,7 @@
         v((2, 64, DI), F32), v((2, NZ, 64, DI), F32),
         v((2, 2, DI, 256), F32), v((2, DI, 256), F32), v((2, DI, 256), F32), v((DI, 256), F32),
         v((2, 64, DI), F32), v((KEYS // 4, DI), F32),
-        dma((6,)), dma((11,)), dma((11,)), dma((5, 7)), dma((5, 7)), dma((7, 7)), dma((7, 7)),
+        dma((6,)), dma((13,)), dma((13,)), dma((5, 7)), dma((5, 7)), dma((7, 7)), dma((7, 7)),
     ]
     grad_queries, grad_keys = pl.pallas_call(
         kernel,

time: 59.1 us -> 61.9 us (1.047)
  Pallas kernels: 58.1 us -> 61.2 us
    pallas_call x1, Pallas kernels: 56.2 us -> 59.3 us  [body(): pl.pallas_call(kernel, out_shape=(jax.ShapeDtypeStruct((Q * JL, DI), F32)...]
where the time goes in v6:
time: 61.9 us; the launch traced here: 61.8 us
  Pallas kernels  61.2 us (99%)
  between operations  0.64 us (1%)
    pallas_call x1, Pallas kernels, body(): pl.pallas_call(kernel, out_shape=(jax.ShapeDtypeStruct((Q * JL, DI), F32)...  59.3 us
    pallas_call x1, Pallas kernels, body(): pl.pallas_call(deliver, out_shape=(jax.ShapeDtypeStruct((Q * JL, DI), F32...  1.91 us

profile of v6, /device:TPU:8, one launch (start us, length us, event | category | flops | bytes accessed | tf_op | source)
XLA Modules:
  0.0 61.8 jit_solution(5569026949170782873)
XLA Ops:
  0.6 59.3 %shard_map.77 = (f32[1024,128]{1,0:T(8,128)}, f32[256,128]{1,0:T(8,128)}) custom-call(s32[64]{0:T(128)} %pos_ref.1, bf16[2048,576]{1,0:T(8,128)(2,1)} %bitcast.5, bf16[576,1024]{1,0:T(8,128)(2,1)} %bitcast.6, bf16[1024,128]{1,0:T(8,128)(2,1)} %bitcast.7, bf16[1024,128]{1,0:T(8,128)(2,1)} %ik_hbm.1, f32[16,64]{1,0:T(8,128)} %bitcast.8), custom_call_target="tpu_custom_call" | custom-call | tf_op jit(solution)/shard_map/pallas_call | solution.py:476
  59.9 1.9 %shard_map.78 = (f32[1024,128]{1,0:T(8,128)}, f32[256,128]{1,0:T(8,128)}) custom-call(f32[1024,128]{1,0:T(8,128)} %get-tuple-element.6.gq_in, f32[256,128]{1,0:T(8,128)} %get-tuple-element.7.gk_in), custom_call_target="tpu_custom_call" | custom-call | tf_op jit(solution)/shard_map/pallas_call | solution.py:496
